TPU v7x, 32 devices: a whole 2x2x4 slice. The times are simulated.
32 devices in a mesh: parts: 2 (over y), graph: 4 (over z), dp: 2 (over x), sub: 2 (over core).
Axes of the slice: x: 2, y: 2, z: 4, core: 2. Of those that a mesh axis runs over, the one named last changes fastest.
Arguments:
- node_feats: bfloat16 [4, 64, 3200], P(('parts', 'dp'), 'graph'), parts along dimension 0, may hold values from -6 to 6
- frame_blocks: bfloat16 [4, 1280, 165], P(('parts', 'dp'), ('graph', 'sub')), parts along dimension 0, may hold values from -4 to 4
- src_ids: int32 [4, 1280], P(('parts', 'dp'), ('graph', 'sub')), parts along dimension 0, may hold values from 0 to 63, as said below
- dst_ids: int32 [4, 1280], P(('parts', 'dp'), ('graph', 'sub')), parts along dimension 0, may hold values from 0 to 63, as said below
- edge_bias: float32 [4, 1280, 8], P(('parts', 'dp'), ('graph', 'sub')), parts along dimension 0, may hold values from -6 to 305
- w_zero: bfloat16 [640, 640], replicated, may hold values from -0.25 to 0.25
- w_one: bfloat16 [2, 512, 512], replicated, may hold values from -0.1875 to 0.1875
- w_two: bfloat16 [2, 384, 384], replicated, may hold values from -0.21875 to 0.21875
- alpha_w: bfloat16 [128, 8], replicated, may hold values from -0.5 to 0.5
- out_proj: bfloat16 [128, 128], replicated, may hold values from -1.5 to 1.5
- grad_out: bfloat16 [4, 64, 3200], P(('parts', 'dp'), 'graph'), parts along dimension 0, may hold values from -6 to 6
Outputs:
- updated: bfloat16 [4, 64, 3200], P(('parts', 'dp'), 'graph'), parts along dimension 0
- grad_nodes: float32 [4, 64, 3200], P(('parts', 'dp'), ('graph', 'sub')), parts along dimension 0
- grad_w_zero: float32 [1280, 640], P(('parts', 'graph', 'sub')), parts along dimension 0
- grad_w_one: float32 [4, 512, 512], P('parts', ('graph', 'sub')), parts along dimension 0
- grad_w_two: float32 [4, 384, 384], P('parts', ('graph', 'sub')), parts along dimension 0
- grad_alpha: float32 [256, 8], P(('parts', 'graph', 'sub')), parts along dimension 0
- grad_proj: float32 [256, 128], P(('parts', 'graph', 'sub')), parts along dimension 0
There are 2 independent parts, one for each index of `parts`. A program takes and returns all parts, laid end to end along the dimension named above; an argument that names none is the same for every part. Nothing has to cross between parts.
Inputs may be any that keep to these rules, and one draw needn't show every extreme that they name: `dst_ids`: edges of a cell are ordered by destination; the edges at positions g * 20 * 16 to (g + 1) * 20 * 16 - 1 point at atoms g * 16 to (g + 1) * 16 - 1, and every atom has at least one edge. `src_ids`: an edge's source lies in the block of 16 atoms of its destination or in the block just before or after it, wrapping around the cell.
All inputs are finite; a program needn't handle non-finite values.
Results may differ from a plain program's by a relative error of at most 0.014.
Values may be sent and summed in bfloat16 or wider, within the bound.
A program may use at most 128 MiB of HBM per device.

v0:
```python
import jax
import jax.numpy as jnp
from jax import lax
from jax.experimental import pallas as pl
from jax.experimental.pallas import tpu as pltpu
from jax.sharding import PartitionSpec as P


def extended(block, sides, width):
    for axis, dim in sides:
        count = lax.axis_size(axis)
        forward = [(i, i + 1) for i in range(count - 1)]
        forward.append((count - 1, 0))
        backward = [(target, source) for source, target in forward]
        low = lax.ppermute(
            lax.slice_in_dim(block, block.shape[dim] - width, None, axis=dim), axis, forward
        )
        high = lax.ppermute(lax.slice_in_dim(block, 0, width, axis=dim), axis, backward)
        block = jnp.concatenate([low, block, high], axis=dim)
    return block


def combined_all(value, axis, join):
    pieces = jax.tree.map(lambda part: lax.all_gather(part, axis), value)
    head = jax.tree.map(lambda part: part[0], pieces)
    tail = jax.tree.map(lambda part: part[1:], pieces)
    running, _ = lax.scan(lambda running, section: (join(running, section), None), head, tail)
    return running


def passed_along(value, axis, by):
    peers = lax.axis_size(axis)
    return lax.ppermute(value, axis, [(i, (i + by) % peers) for i in range(peers)])


def contract(form, left, right):
    if left.dtype == right.dtype:
        return jnp.einsum(
            form, left, right, preferred_element_type=jnp.float32, precision=lax.Precision.HIGHEST
        )
    return jnp.einsum(form, left.astype(jnp.float32), right, precision=lax.Precision.HIGHEST)


def inner(left, right):
    return lax.dot_general(
        left, right, (((0,), (0,)), ((), ())), preferred_element_type=jnp.float32
    )


def across(left, right):
    return lax.dot_general(
        left, right, (((1,), (1,)), ((), ())), preferred_element_type=jnp.float32
    )


def frame_pieces(frames):
    pieces = []
    offset = 0
    for degree in range(5):
        breadth = 2 * degree + 1
        square = frames[:, offset : offset + breadth * breadth].reshape(-1, breadth, breadth)
        offset = offset + breadth * breadth
        reach = min(degree, 2)
        pieces.append(square[:, degree - reach : degree + reach + 1, :])
    return pieces


def degree_slice(matrix, degree, channels):
    return matrix[:, degree * degree * channels : (degree + 1) * (degree + 1) * channels].reshape(
        matrix.shape[0], 2 * degree + 1, channels
    )


def group_coeffs(pieces):
    centre = [min(degree, 2) for degree in range(5)]
    order_zero = jnp.concatenate(
        [pieces[degree][:, centre[degree], :] for degree in range(5)], axis=1
    )
    order_one = jnp.concatenate(
        [pieces[degree][:, centre[degree] + 1, :] for degree in range(1, 5)]
        + [pieces[degree][:, centre[degree] - 1, :] for degree in range(1, 5)],
        axis=1,
    )
    order_two = jnp.concatenate(
        [pieces[degree][:, 4, :] for degree in range(2, 5)]
        + [pieces[degree][:, 0, :] for degree in range(2, 5)],
        axis=1,
    )
    return (order_zero, order_one, order_two)


def split_coeffs(order_zero, order_one, order_two, breadth):
    pieces = []
    for degree in range(5):
        stacked = [order_zero[:, degree * breadth : (degree + 1) * breadth]]
        if degree >= 1:
            stacked = (
                [order_one[:, (3 + degree) * breadth : (4 + degree) * breadth]]
                + stacked
                + [order_one[:, (degree - 1) * breadth : degree * breadth]]
            )
        if degree >= 2:
            stacked = (
                [order_two[:, (1 + degree) * breadth : (2 + degree) * breadth]]
                + stacked
                + [order_two[:, (degree - 2) * breadth : (degree - 1) * breadth]]
            )
        pieces.append(jnp.stack(stacked, axis=1))
    return pieces


def pair_matrix(weights):
    real_part = weights[0]
    imag_part = weights[1]
    return jnp.concatenate(
        [
            jnp.concatenate([real_part, imag_part], axis=1),
            jnp.concatenate([-imag_part, real_part], axis=1),
        ],
        axis=0,
    )


def spread_heads(weights, value_ch):
    return jnp.repeat(weights, value_ch // weights.shape[1], axis=1)


def spread_rows(factor, value_ch):
    return jnp.tile(spread_heads(factor, value_ch), (1, 25))


def edge_forward(source_rows, pieces, w_zero, w_one, w_two, alpha_w, edge_bias):
    channels = source_rows.shape[1] // 25
    value_ch = w_zero.shape[1] // 5
    rotated = [
        contract(
            "ekm,emc->ekc", pieces[degree], degree_slice(source_rows, degree, channels)
        ).astype(jnp.bfloat16)
        for degree in range(5)
    ]
    inputs = group_coeffs(rotated)
    out_zero = jnp.dot(inputs[0], w_zero, preferred_element_type=jnp.float32)
    out_one = jnp.dot(inputs[1], pair_matrix(w_one), preferred_element_type=jnp.float32)
    out_two = jnp.dot(inputs[2], pair_matrix(w_two), preferred_element_type=jnp.float32)
    scalar = out_zero[:, :value_ch]
    gate = jax.nn.silu(scalar).astype(jnp.bfloat16)
    logits = jnp.dot(gate, alpha_w, preferred_element_type=jnp.float32) + edge_bias
    values = split_coeffs(
        out_zero.astype(jnp.bfloat16),
        out_one.astype(jnp.bfloat16),
        out_two.astype(jnp.bfloat16),
        value_ch,
    )
    return (inputs, scalar, gate, logits, values)


def rotate_back(weights, values, pieces):
    value_ch = values[0].shape[2]
    spread = spread_heads(weights, value_ch)[:, None, :]
    outputs = [
        contract("ekm,ekv->emv", pieces[degree], values[degree].astype(jnp.float32) * spread)
        for degree in range(5)
    ]
    return jnp.concatenate([item.reshape(item.shape[0], -1) for item in outputs], axis=1)


def attention_grads(grad_back, values, pieces, heads):
    value_ch = values[0].shape[2]
    message_grads = [
        contract("ekm,emv->ekv", pieces[degree], degree_slice(grad_back, degree, value_ch))
        for degree in range(5)
    ]
    product = jnp.sum(message_grads[0] * values[0].astype(jnp.float32), axis=1)
    for degree in range(1, 5):
        product = product + jnp.sum(
            message_grads[degree] * values[degree].astype(jnp.float32), axis=1
        )
    head_grad = product.reshape(product.shape[0], heads, value_ch // heads).sum(axis=2)
    return (message_grads, head_grad)


def value_grads(message_grads, attention, logit_grad, scalar, alpha_w):
    value_ch = scalar.shape[1]
    spread = spread_heads(attention, value_ch)[:, None, :]
    grads = [item * spread for item in message_grads]
    order_zero, order_one, order_two = group_coeffs(grads)
    sigmoid = jax.nn.sigmoid(scalar)
    gate_grad = across(logit_grad, alpha_w) * sigmoid * (1.0 + scalar * (1.0 - sigmoid))
    order_zero = jnp.concatenate(
        [order_zero[:, :value_ch] + gate_grad, order_zero[:, value_ch:]], axis=1
    )
    return (
        order_zero.astype(jnp.bfloat16),
        order_one.astype(jnp.bfloat16),
        order_two.astype(jnp.bfloat16),
    )


def pair_grad(block, half_in, half_out):
    return jnp.stack(
        [
            block[:half_in, :half_out] + block[half_in:, half_out:],
            block[:half_in, half_out:] - block[half_in:, :half_out],
        ]
    )


def input_grads(inputs, grads, w_zero, w_one, w_two, pieces, channels):
    weight_zero = inner(inputs[0], grads[0])
    weight_one = pair_grad(inner(inputs[1], grads[1]), w_one.shape[1], w_one.shape[2])
    weight_two = pair_grad(inner(inputs[2], grads[2]), w_two.shape[1], w_two.shape[2])
    coeff_zero = across(grads[0], w_zero).astype(jnp.bfloat16)
    coeff_one = across(grads[1], pair_matrix(w_one)).astype(jnp.bfloat16)
    coeff_two = across(grads[2], pair_matrix(w_two)).astype(jnp.bfloat16)
    coeff_pieces = split_coeffs(coeff_zero, coeff_one, coeff_two, channels)
    row_grads = jnp.concatenate(
        [
            contract("ekm,ekc->emc", pieces[degree], coeff_pieces[degree]).reshape(
                coeff_zero.shape[0], -1
            )
            for degree in range(5)
        ],
        axis=1,
    )
    return ((weight_zero, weight_one, weight_two), row_grads)


def grouped_rows(item, groups):
    if item.ndim == 3:
        return jnp.transpose(
            item.reshape(2, groups, item.shape[1] // groups, item.shape[2]), (1, 0, 2, 3)
        ).reshape(groups, -1)
    return item.reshape(groups, -1)


def body(
    node_feats,
    frame_blocks,
    src_ids,
    dst_ids,
    edge_bias,
    w_zero,
    w_one,
    w_two,
    alpha_w,
    out_proj,
    grad_out,
):
    tile_rows = node_feats.shape[1]
    channels = node_feats.shape[2] // 25
    value_ch = w_zero.shape[1] // 5
    heads = alpha_w.shape[1]
    owners = lax.axis_size("graph")
    owner = lax.axis_index("graph")
    padded = extended(node_feats, (("graph", 1),), tile_rows)[0]
    sources = src_ids[0]
    targets = dst_ids[0] - owner * tile_rows
    slots = (sources // tile_rows - owner + 1 + owners) % owners * tile_rows + sources % tile_rows
    pieces = frame_pieces(frame_blocks[0])
    source_rows = jnp.take(padded, slots, axis=0)
    inputs, scalar, gate, logits, values = edge_forward(
        source_rows, pieces, w_zero, w_one, w_two, alpha_w, edge_bias[0]
    )
    local_max = jnp.maximum(
        jax.ops.segment_max(logits, targets, num_segments=tile_rows, indices_are_sorted=True), -1e30
    )
    raised = jnp.exp(logits - local_max[targets])
    local_total = jax.ops.segment_sum(
        raised, targets, num_segments=tile_rows, indices_are_sorted=True
    )
    local_acc = jax.ops.segment_sum(
        rotate_back(raised, values, pieces),
        targets,
        num_segments=tile_rows,
        indices_are_sorted=True,
    )

    def combine(earlier, later):
        highest = jnp.maximum(earlier[0], later[0])
        left_scale = jnp.exp(earlier[0] - highest)
        right_scale = jnp.exp(later[0] - highest)
        return (
            highest,
            earlier[1] * left_scale + later[1] * right_scale,
            earlier[2] * spread_rows(left_scale, value_ch)
            + later[2] * spread_rows(right_scale, value_ch),
        )

    highest, totals, summed = combined_all((local_max, local_total, local_acc), "sub", combine)
    summed_half = (summed / spread_rows(totals, value_ch)).astype(jnp.bfloat16)
    attention = jnp.exp(logits - highest[targets]) / totals[targets]
    own_rows = node_feats[0]
    projected = jnp.dot(
        summed_half.reshape(-1, value_ch), out_proj, preferred_element_type=jnp.float32
    ).reshape(tile_rows, -1)
    updated = (own_rows.astype(jnp.float32) + projected).astype(jnp.bfloat16)
    own_grad = grad_out[0]
    half_rows = tile_rows // lax.axis_size("sub")
    half_start = lax.axis_index("sub") * half_rows
    summed_share = lax.dynamic_slice_in_dim(summed_half, half_start, half_rows, 0)
    grad_share = lax.dynamic_slice_in_dim(own_grad, half_start, half_rows, 0)
    proj_grad = inner(summed_share.reshape(-1, value_ch), grad_share.reshape(-1, channels))
    summed_grad = across(own_grad.reshape(-1, channels), out_proj).reshape(tile_rows, -1)
    message_grads, head_grad = attention_grads(summed_grad[targets], values, pieces, heads)
    local_dots = jax.ops.segment_sum(
        attention * head_grad, targets, num_segments=tile_rows, indices_are_sorted=True
    )
    dots = lax.psum(local_dots, "sub")
    logit_grad = (attention * (head_grad - dots[targets])).astype(jnp.bfloat16)
    alpha_grad = inner(gate, logit_grad)
    grads = value_grads(message_grads, attention, logit_grad, scalar, alpha_w)
    conv_grads, row_grads = input_grads(inputs, grads, w_zero, w_one, w_two, pieces, channels)
    buffer_grads = jax.ops.segment_sum(row_grads, slots, num_segments=3 * tile_rows)
    from_after = passed_along(buffer_grads[:tile_rows].astype(jnp.bfloat16), "graph", -1).astype(
        jnp.float32
    )
    from_before = passed_along(
        buffer_grads[2 * tile_rows :].astype(jnp.bfloat16), "graph", 1
    ).astype(jnp.float32)
    own_total = buffer_grads[tile_rows : 2 * tile_rows] + from_after + from_before
    node_share = lax.psum_scatter(
        own_total.astype(jnp.bfloat16), "sub", scatter_dimension=0, tiled=True
    ).astype(jnp.float32)
    grad_nodes = node_share + grad_share.astype(jnp.float32)
    terms = conv_grads + (alpha_grad, proj_grad)
    groups = lax.axis_size("graph") * lax.axis_size("sub")
    flattened = jnp.concatenate([grouped_rows(item, groups) for item in terms], axis=1)
    share = lax.psum_scatter(
        flattened.astype(jnp.bfloat16), ("graph", "sub"), scatter_dimension=0, tiled=True
    ).astype(jnp.float32)
    share = lax.psum(share.astype(jnp.bfloat16), "dp").astype(jnp.float32)[0]
    results = []
    offset = 0
    for item in terms:
        count = item.size // groups
        piece = share[offset : offset + count]
        if item.ndim == 3:
            results.append(piece.reshape(2, item.shape[1] // groups, item.shape[2]))
        else:
            results.append(piece.reshape(item.shape[0] // groups, item.shape[1]))
        offset = offset + count
    return (
        updated[None],
        grad_nodes[None],
        results[0],
        results[1],
        results[2],
        results[3],
        results[4],
    )


def column(degree, order):
    if order == 0:
        return degree
    if order == 1:
        return 5 + degree - 1
    if order == -1:
        return 9 + degree - 1
    if order == 2:
        return 13 + degree - 2
    return 16 + degree - 2


def frame_entries():
    entries = []
    offset = 0
    for degree in range(5):
        breadth = 2 * degree + 1
        reach = min(degree, 2)
        for order in range(-reach, reach + 1):
            for full in range(breadth):
                entries.append((degree, order, full, offset + (degree + order) * breadth + full))
        offset += breadth * breadth
    return entries


ENTRIES = frame_entries()
INDEX = {(d, o, f): i for i, (d, o, f, _) in enumerate(ENTRIES)}
LANES = 128
STEP = 16
F32 = jnp.float32
BF16 = jnp.bfloat16


def exact(left, right):
    return jnp.dot(left, right, preferred_element_type=F32, precision=lax.Precision.HIGHEST)


def fast(left, right):
    return jnp.dot(left, right, preferred_element_type=F32)


def lanes(index, count=1):
    return slice(index * LANES, (index + count) * LANES)


def fused(
    graphs, dps, parts,
    nf, fr, src, dst, bias, w0, w1, w2, aw, op, go,
    upd, gn, o0, o1, o2, oa, oproj,
    halo, small, small_in, acc_out, acc_in, fb, gp, sr, mg, zz, vv, weight, bk, gg, ig, rg, ng, ng_in,
    wg, r1, hh, r2, kk, r3, fin,
    halo_send, halo_recv, small_send, small_recv, acc_send, acc_recv, ng_send, ng_recv,
    s1s, s1r, s2s, s2r, s3s, s3r, s4s, s4r,
):
    edges = fr.shape[0]
    rows_dev = nf.shape[0]
    heads = aw.shape[1]
    g = lax.axis_index("graph")
    s = lax.axis_index("sub")
    d = lax.axis_index("dp")
    other = 1 - s

    def along(k):
        return lax.rem(g + k + graphs, graphs)

    def dp_along(k):
        return lax.rem(d + k, dps)

    def remote(source, target, send, recv, device):
        return pltpu.make_async_remote_copy(
            src_ref=source, dst_ref=target, send_sem=send, recv_sem=recv,
            device_id=device, device_id_type=pl.DeviceIdType.MESH,
        )

    barrier = pltpu.get_barrier_semaphore()
    peers = [{"sub": other}]
    for k in range(1, graphs):
        peers.append({"graph": along(k)})
    peers.append({"graph": along(1), "sub": other})
    peers.append({"graph": along(-1), "sub": other})
    for k in range(1, dps):
        peers.append({"dp": dp_along(k)})
    for peer in peers:
        pl.semaphore_signal(barrier, inc=1, device_id=peer, device_id_type=pl.DeviceIdType.MESH)
    pl.semaphore_wait(barrier, len(peers))

    halo_up = remote(nf, halo.at[0], halo_send.at[0], halo_recv.at[0], {"graph": along(1)})
    halo_down = remote(nf, halo.at[1], halo_send.at[1], halo_recv.at[1], {"graph": along(-1)})
    halo_up.start()
    halo_down.start()

    src_row = src[...]
    dst_row = dst[...]
    eye = lax.broadcasted_iota(jnp.int32, (edges, edges), 0) == lax.broadcasted_iota(
        jnp.int32, (edges, edges), 1
    )

    def to_column(row):
        spread = jnp.where(eye, jnp.broadcast_to(row.astype(F32), (edges, edges)), 0.0)
        return jnp.sum(spread, axis=1, keepdims=True).astype(jnp.int32)

    src_col = to_column(src_row)
    dst_col = to_column(dst_row) - g * rows_dev
    lane48 = lax.broadcasted_iota(jnp.int32, (edges, 3 * rows_dev), 1)
    row48 = lax.broadcasted_iota(jnp.int32, (3 * rows_dev, edges), 0)

    def block_ids(position):
        low = along(-1) * rows_dev + position
        mid = g * rows_dev + position - rows_dev
        high = along(1) * rows_dev + position - 2 * rows_dev
        return jnp.where(
            position < rows_dev, low, jnp.where(position < 2 * rows_dev, mid, high)
        )

    def hot(match, dtype=BF16):
        return jnp.where(match, 1.0, 0.0).astype(dtype)

    pick_src = hot(block_ids(lane48) == src_col)
    put_src = hot(block_ids(row48) == src_row)
    pick_dst = hot(lax.broadcasted_iota(jnp.int32, (edges, rows_dev), 1) == dst_col)
    put_dst = hot(
        lax.broadcasted_iota(jnp.int32, (rows_dev, edges), 0) == dst_row - g * rows_dev
    )
    lane_j = lax.broadcasted_iota(jnp.int32, (edges, LANES), 1)
    mine = lax.shift_right_logical(lane_j, 3) == dst_col
    sq0 = lax.broadcasted_iota(jnp.int32, (LANES, LANES), 0)
    sq1 = lax.broadcasted_iota(jnp.int32, (LANES, LANES), 1)
    spread = hot(jnp.bitwise_and(sq0, 7) == lax.shift_right_logical(sq1, 4), F32)
    gather_heads = hot(lax.shift_right_logical(sq0, 4) == jnp.bitwise_and(sq1, 7), F32)
    compact = hot(jnp.bitwise_and(sq0, 7) == sq1)
    tile_heads = hot(
        lax.broadcasted_iota(jnp.int32, (heads, LANES), 0)
        == jnp.bitwise_and(lax.broadcasted_iota(jnp.int32, (heads, LANES), 1), 7),
        F32,
    )
    alpha_t = fast(aw[...], tile_heads.astype(BF16)).astype(BF16)
    proj = op[...]

    for k in range(25):
        rows = fast(pick_dst, go[:, lanes(k)]).astype(BF16)
        gp[:, lanes(k)] = across(rows, proj)

    def message_step(c, _):
        at = pl.ds(pl.multiple_of(c * STEP, STEP), STEP)
        frames = fr[at, :].astype(F32)
        for degree in range(5):
            reach = min(degree, 2)
            breadth = 2 * degree + 1
            inputs = [gp[at, lanes(degree * degree + f)] for f in range(breadth)]
            for order in range(-reach, reach + 1):
                total = None
                for f in range(breadth):
                    i = INDEX[(degree, order, f)]
                    col = ENTRIES[i][3]
                    value = jnp.broadcast_to(frames[:, col : col + 1], (STEP, LANES))
                    fb[i, at, :] = value
                    term = value * inputs[f]
                    total = term if total is None else total + term
                mg[at, lanes(column(degree, order))] = total
        return 0

    lax.fori_loop(0, edges // STEP, message_step, 0)

    halo_up.wait()
    halo_down.wait()
    for k in range(25):
        block = jnp.concatenate([halo[0, :, lanes(k)], nf[:, lanes(k)], halo[1, :, lanes(k)]], axis=0)
        sr[:, lanes(k)] = fast(pick_src, block)

    def rotate_step(c, _):
        at = pl.ds(pl.multiple_of(c * STEP, STEP), STEP)
        for degree in range(5):
            reach = min(degree, 2)
            breadth = 2 * degree + 1
            inputs = [sr[at, lanes(degree * degree + f)] for f in range(breadth)]
            for order in range(-reach, reach + 1):
                total = None
                for f in range(breadth):
                    term = fb[INDEX[(degree, order, f)], at, :] * inputs[f]
                    total = term if total is None else total + term
                zz[at, lanes(column(degree, order))] = total.astype(BF16)
        return 0

    lax.fori_loop(0, edges // STEP, rotate_step, 0)

    z0 = zz[:, lanes(0, 5)]
    zp1, zm1 = zz[:, lanes(5, 4)], zz[:, lanes(9, 4)]
    zp2, zm2 = zz[:, lanes(13, 3)], zz[:, lanes(16, 3)]
    y0 = fast(z0, w0[...])
    scalar = y0[:, :LANES]
    vv[:, lanes(0, 5)] = y0.astype(BF16)
    vv[:, lanes(5, 4)] = (fast(zp1, w1[0]) - fast(zm1, w1[1])).astype(BF16)
    vv[:, lanes(9, 4)] = (fast(zp1, w1[1]) + fast(zm1, w1[0])).astype(BF16)
    vv[:, lanes(13, 3)] = (fast(zp2, w2[0]) - fast(zm2, w2[1])).astype(BF16)
    vv[:, lanes(16, 3)] = (fast(zp2, w2[1]) + fast(zm2, w2[0])).astype(BF16)
    sigmoid = lax.logistic(scalar)
    gate = (scalar * sigmoid).astype(BF16)
    logits = fast(gate, alpha_t) + exact(bias[...], tile_heads)
    logits = jnp.where(mine, logits, -1e30)
    product = None
    for k in range(19):
        term = mg[:, lanes(k)] * vv[:, lanes(k)].astype(F32)
        product = term if product is None else product + term
    head_grad = exact(product, gather_heads)
    peak = jnp.max(logits, axis=0, keepdims=True)
    raised = jnp.where(mine, jnp.exp(logits - peak), 0.0)
    total = jnp.sum(raised, axis=0, keepdims=True)
    dots = jnp.sum(raised * head_grad, axis=0, keepdims=True)
    small[0:1, :] = peak
    small[1:2, :] = total
    small[2:3, :] = dots
    small[3:8, :] = jnp.zeros((5, LANES), F32)
    small_copy = remote(small, small_in, small_send, small_recv, {"sub": other})
    small_copy.start()

    weight[...] = exact(raised, spread)

    def back_step(c, _):
        at = pl.ds(pl.multiple_of(c * STEP, STEP), STEP)
        scale = weight[at, :]
        for degree in range(5):
            reach = min(degree, 2)
            orders = range(-reach, reach + 1)
            inputs = {o: vv[at, lanes(column(degree, o))].astype(F32) * scale for o in orders}
            for f in range(2 * degree + 1):
                out = None
                for o in orders:
                    term = fb[INDEX[(degree, o, f)], at, :] * inputs[o]
                    out = term if out is None else out + term
                bk[at, lanes(degree * degree + f)] = out.astype(BF16)
        return 0

    lax.fori_loop(0, edges // STEP, back_step, 0)
    small_copy.wait()
    peak_in = small_in[0:1, :]
    top = jnp.maximum(peak, peak_in)
    own_scale = jnp.exp(peak - top)
    in_scale = jnp.exp(peak_in - top)
    whole = total * own_scale + small_in[1:2, :] * in_scale
    all_dots = (dots * own_scale + small_in[2:3, :] * in_scale) / whole
    node_lane = lax.broadcasted_iota(jnp.int32, (rows_dev, LANES), 1)
    node_row = lax.broadcasted_iota(jnp.int32, (rows_dev, LANES), 0)
    node_scale = exact(
        jnp.where(lax.shift_right_logical(node_lane, 3) == node_row, own_scale / whole, 0.0), spread
    )
    for k in range(25):
        acc_out[:, lanes(k)] = fast(put_dst, bk[:, lanes(k)]) * node_scale
    acc_copy = remote(acc_out, acc_in, acc_send, acc_recv, {"sub": other})
    acc_copy.start()

    attention = raised * (own_scale / whole)
    logit_grad = (attention * (head_grad - all_dots)).astype(BF16)
    spread_att = exact(attention, spread)
    gate_grad = across(logit_grad, alpha_t) * sigmoid * (1.0 + scalar * (1.0 - sigmoid))
    for k in range(19):
        grad = mg[:, lanes(k)] * spread_att
        if k == 0:
            grad = grad + gate_grad
        gg[:, lanes(k)] = grad.astype(BF16)

    groups = graphs * 2

    def put(piece, base, rows_share, row0, matrix):
        wide = matrix.shape[1] // LANES
        part = wg[piece].shape[3]
        for i in range(matrix.shape[0] // STEP):
            row = row0 + i * STEP
            group = row // rows_share
            inner_row = (row % rows_share) // STEP
            for j in range(wide):
                tile = base + inner_row * wide + j
                wg[piece][group % 2, tile // part, group // 2, tile % part] = matrix[
                    i * STEP : (i + 1) * STEP, lanes(j)
                ].astype(BF16)

    def zero_tail(piece, used):
        part = wg[piece].shape[3]
        for tile in range(used, part * dps):
            wg[piece][:, tile // part, :, tile % part] = jnp.zeros((2, graphs, STEP, LANES), BF16)

    def stage_one(piece):
        return remote(
            wg[piece].at[other], r1[piece], s1s.at[piece], s1r.at[piece], {"sub": other}
        )

    def stage_two(piece):
        return [
            remote(
                hh[piece].at[dp_along(k)], r2[piece].at[k - 1],
                s2s.at[piece, k - 1], s2r.at[piece, k - 1], {"dp": dp_along(k)},
            )
            for k in range(1, dps)
        ]

    def stage_three(piece):
        return [
            remote(
                kk[piece].at[along(k)], r3[piece].at[k - 1],
                s3s.at[piece, k - 1], s3r.at[piece, k - 1], {"graph": along(k)},
            )
            for k in range(1, graphs)
        ]

    def stage_four(piece):
        return [
            remote(
                fin[piece].at[0], fin[piece].at[k],
                s4s.at[piece, k - 1], s4r.at[piece, k - 1], {"dp": dp_along(k)},
            )
            for k in range(1, dps)
        ]

    def start(copies):
        for copy in copies:
            copy.start()
        return copies

    def wait(copies):
        for copy in copies:
            copy.wait()

    gp1, gm1 = gg[:, lanes(5, 4)], gg[:, lanes(9, 4)]
    rows1 = 512 // groups
    for b in range(4):
        zp, zm = zz[:, lanes(5 + b)], zz[:, lanes(9 + b)]
        base = (rows1 // STEP) * 4
        put(0, 0, rows1, b * LANES, inner(zp, gp1) + inner(zm, gm1))
        put(0, base, rows1, b * LANES, inner(zp, gm1) - inner(zm, gp1))
    zero_tail(0, 2 * (rows1 // STEP) * 4)
    one = [None] * 3
    one[0] = stage_one(0)
    one[0].start()

    g0 = gg[:, lanes(0, 5)]
    rows0 = 640 // groups
    for b in range(5):
        put(1, 0, rows0, b * LANES, inner(zz[:, lanes(b)], g0))
    alpha_rows = LANES // groups
    tiles0 = (rows0 // STEP) * 5
    logit_small = fast(logit_grad, compact).astype(BF16)
    put(1, tiles0, alpha_rows, 0, inner(gate, logit_small))
    zero_tail(1, tiles0 + alpha_rows // STEP)
    one[1] = stage_one(1)
    one[1].start()

    acc_copy.wait()
    summed = jnp.concatenate(
        [(acc_out[:, lanes(k)] + acc_in[:, lanes(k)]).astype(BF16) for k in range(25)], axis=0
    )
    projected = fast(summed, proj)
    for k in range(25):
        upd[:, lanes(k)] = (
            nf[:, lanes(k)].astype(F32) + projected[k * rows_dev : (k + 1) * rows_dev]
        ).astype(BF16)
    cotangent = jnp.concatenate([go[:, lanes(k)] for k in range(25)], axis=0)
    half = rows_dev // 2
    in_half = lax.broadcasted_iota(jnp.int32, summed.shape, 0)
    in_half = lax.shift_right_logical(jnp.bitwise_and(in_half, rows_dev - 1), 3) == s
    share = jnp.where(in_half, summed.astype(F32), 0.0).astype(BF16)
    gp2, gm2 = gg[:, lanes(13, 3)], gg[:, lanes(16, 3)]
    rows2 = 384 // groups
    tiles2 = (rows2 // STEP) * 3
    for b in range(3):
        zp, zm = zz[:, lanes(13 + b)], zz[:, lanes(16 + b)]
        put(2, 0, rows2, b * LANES, inner(zp, gp2) + inner(zm, gm2))
        put(2, tiles2, rows2, b * LANES, inner(zp, gm2) - inner(zm, gp2))
    put(2, 2 * tiles2, alpha_rows, 0, inner(share, cotangent))
    zero_tail(2, 2 * tiles2 + alpha_rows // STEP)
    one[2] = stage_one(2)
    one[2].start()

    def add_one(piece):
        one[piece].wait()
        for p in range(dps):
            hh[piece][p] = (wg[piece][s, p].astype(F32) + r1[piece][p].astype(F32)).astype(BF16)
        return start(stage_two(piece))

    def add_two(piece):
        wait(two[piece])
        value = hh[piece][d].astype(F32)
        for k in range(1, dps):
            value = value + r2[piece][k - 1].astype(F32)
        kk[piece][...] = value.astype(BF16)
        return start(stage_three(piece))

    def add_three(piece):
        wait(three[piece])
        value = kk[piece][g].astype(F32)
        for k in range(1, graphs):
            value = value + r3[piece][k - 1].astype(F32)
        fin[piece][0] = value.astype(BF16)
        return start(stage_four(piece))

    two = [None] * 3
    three = [None] * 3
    four = [None] * 3
    two[0] = add_one(0)
    two[1] = add_one(1)

    ig[:, lanes(0, 5)] = across(g0, w0[...]).astype(BF16)
    ig[:, lanes(5, 4)] = (across(gp1, w1[0]) + across(gm1, w1[1])).astype(BF16)
    ig[:, lanes(9, 4)] = (across(gm1, w1[0]) - across(gp1, w1[1])).astype(BF16)
    two[2] = add_one(2)
    ig[:, lanes(13, 3)] = (across(gp2, w2[0]) + across(gm2, w2[1])).astype(BF16)
    ig[:, lanes(16, 3)] = (across(gm2, w2[0]) - across(gp2, w2[1])).astype(BF16)

    def row_step(c, _):
        at = pl.ds(pl.multiple_of(c * STEP, STEP), STEP)
        for degree in range(5):
            reach = min(degree, 2)
            orders = range(-reach, reach + 1)
            inputs = {o: ig[at, lanes(column(degree, o))].astype(F32) for o in orders}
            for f in range(2 * degree + 1):
                out = None
                for o in orders:
                    term = fb[INDEX[(degree, o, f)], at, :] * inputs[o]
                    out = term if out is None else out + term
                rg[at, lanes(degree * degree + f)] = out.astype(BF16)
        return 0

    lax.fori_loop(0, edges // STEP, row_step, 0)

    for k in range(13):
        low = fast(put_src, rg[:, lanes(k)])
        high = fast(put_src, rg[:, lanes(13 + k)]) if k < 12 else jnp.zeros_like(low)
        for b in range(3):
            for h in range(2):
                at = slice(b * rows_dev + h * half, b * rows_dev + (h + 1) * half)
                ng[b, h, :, lanes(k)] = jnp.concatenate([low[at], high[at]], axis=0).astype(BF16)
    node_copies = []
    for b in range(3):
        for r in range(2):
            if b == 1 and r == 0:
                continue
            to = lax.rem(s + r, 2)
            node_copies.append(
                remote(
                    ng.at[b, to], ng_in.at[b, r], ng_send.at[b, r], ng_recv.at[b, r],
                    {"graph": along(b - 1), "sub": to},
                )
            )
    start(node_copies)

    three[0] = add_two(0)
    three[1] = add_two(1)
    three[2] = add_two(2)

    wait(node_copies)
    for k in range(13):
        value = ng[1, s, :, lanes(k)].astype(F32)
        for b in range(3):
            for r in range(2):
                if b == 1 and r == 0:
                    continue
                value = value + ng_in[b, r, :, lanes(k)].astype(F32)
        for part, coef in ((0, k), (1, 13 + k)):
            if coef < 25:
                base = go[:, lanes(coef)].astype(F32)
                base = jnp.where(s == 0, base[:half], base[half:])
                gn[:, lanes(coef)] = value[part * half : (part + 1) * half] + base

    def take(piece, tile):
        part = fin[piece].shape[1]
        slot = lax.rem(d - tile // part + dps, dps)
        return fin[piece][slot, tile % part].astype(F32)

    four[0] = add_three(0)
    four[1] = add_three(1)
    wait(four[0])
    for q in range(2):
        for i in range(rows1 // STEP):
            for j in range(4):
                tile = q * (rows1 // STEP) * 4 + i * 4 + j
                o1[q, i * STEP : (i + 1) * STEP, lanes(j)] = take(0, tile)
    wait(four[1])
    for i in range(rows0 // STEP):
        for j in range(5):
            o0[i * STEP : (i + 1) * STEP, lanes(j)] = take(1, i * 5 + j)
    for i in range(alpha_rows // STEP):
        oa[i * STEP : (i + 1) * STEP, :] = take(1, tiles0 + i)[:, :heads]
    four[2] = add_three(2)
    wait(four[2])
    for q in range(2):
        for i in range(rows2 // STEP):
            for j in range(3):
                o2[q, i * STEP : (i + 1) * STEP, lanes(j)] = take(2, q * tiles2 + i * 3 + j)
    for i in range(alpha_rows // STEP):
        oproj[i * STEP : (i + 1) * STEP, :] = take(2, 2 * tiles2 + i)


def fused_body(graphs, dps, parts):
    groups = graphs * 2

    def run(node_feats, frame_blocks, src_ids, dst_ids, edge_bias, w_zero, w_one, w_two, alpha_w, out_proj, grad_out):
        rows_dev = node_feats.shape[1]
        edges = frame_blocks.shape[1]
        heads = alpha_w.shape[1]
        used = (
            2 * (512 // groups // STEP) * 4,
            (640 // groups // STEP) * 5 + LANES // groups // STEP,
            2 * (384 // groups // STEP) * 3 + LANES // groups // STEP,
        )
        part = [-(-count // dps) for count in used]
        dma = pltpu.SemaphoreType.DMA
        wide = 25 * LANES
        kept = 19 * LANES

        def per_piece(lead):
            return [pltpu.VMEM((*lead(p), STEP, LANES), BF16) for p in part]

        scratch = [
            pltpu.VMEM((2, rows_dev, wide), BF16),
            pltpu.VMEM((8, LANES), F32),
            pltpu.VMEM((8, LANES), F32),
            pltpu.VMEM((rows_dev, wide), F32),
            pltpu.VMEM((rows_dev, wide), F32),
            pltpu.VMEM((len(ENTRIES), edges, LANES), F32),
            pltpu.VMEM((edges, wide), F32),
            pltpu.VMEM((edges, wide), F32),
            pltpu.VMEM((edges, kept), F32),
            pltpu.VMEM((edges, kept), BF16),
            pltpu.VMEM((edges, kept), BF16),
            pltpu.VMEM((edges, LANES), F32),
            pltpu.VMEM((edges, wide), BF16),
            pltpu.VMEM((edges, kept), BF16),
            pltpu.VMEM((edges, kept), BF16),
            pltpu.VMEM((edges, wide), BF16),
            pltpu.VMEM((3, 2, STEP, 13 * LANES), BF16),
            pltpu.VMEM((3, 2, STEP, 13 * LANES), BF16),
            per_piece(lambda p: (2, dps, graphs, p)),
            per_piece(lambda p: (dps, graphs, p)),
            per_piece(lambda p: (dps, graphs, p)),
            per_piece(lambda p: (max(dps - 1, 1), graphs, p)),
            per_piece(lambda p: (graphs, p)),
            per_piece(lambda p: (graphs - 1, p)),
            per_piece(lambda p: (dps, p)),
            dma((2,)), dma((2,)), dma, dma, dma, dma, dma((3, 2)), dma((3, 2)),
            dma((3,)), dma((3,)),
            dma((3, max(dps - 1, 1))), dma((3, max(dps - 1, 1))),
            dma((3, graphs - 1)), dma((3, graphs - 1)),
            dma((3, max(dps - 1, 1))), dma((3, max(dps - 1, 1))),
        ]
        flat = []
        counts = []
        for item in scratch:
            if isinstance(item, list):
                counts.append(len(item))
                flat.extend(item)
            else:
                counts.append(0)
                flat.append(item)

        def entry(*refs):
            lead, rest = refs[:18], list(refs[18:])
            grouped = []
            for count in counts:
                if count:
                    grouped.append(rest[:count])
                    rest = rest[count:]
                else:
                    grouped.append(rest.pop(0))
            fused(graphs, dps, parts, *lead, *grouped)

        vmem = pl.BlockSpec(memory_space=pltpu.VMEM)
        out = pl.pallas_call(
            entry,
            out_shape=(
                jax.ShapeDtypeStruct((rows_dev, wide), BF16),
                jax.ShapeDtypeStruct((rows_dev // 2, wide), F32),
                jax.ShapeDtypeStruct((640 // groups, 640), F32),
                jax.ShapeDtypeStruct((2, 512 // groups, 512), F32),
                jax.ShapeDtypeStruct((2, 384 // groups, 384), F32),
                jax.ShapeDtypeStruct((LANES // groups, heads), F32),
                jax.ShapeDtypeStruct((LANES // groups, LANES), F32),
            ),
            in_specs=[vmem] * 11,
            out_specs=[vmem] * 7,
            scratch_shapes=flat,
            compiler_params=pltpu.CompilerParams(
                collective_id=0, has_side_effects=True, vmem_limit_bytes=56 * 1024 * 1024
            ),
        )(
            node_feats[0], frame_blocks[0], src_ids, dst_ids, edge_bias[0],
            w_zero, w_one, w_two, alpha_w, out_proj, grad_out[0],
        )
        return (out[0][None], out[1][None], *out[2:])

    return run


def solution(mesh):
    placed = (
        P(("parts", "dp"), "graph", None),
        P(("parts", "dp"), ("graph", "sub"), None),
        P(("parts", "dp"), ("graph", "sub")),
        P(("parts", "dp"), ("graph", "sub")),
        P(("parts", "dp"), ("graph", "sub"), None),
        P(),
        P(),
        P(),
        P(),
        P(),
        P(("parts", "dp"), "graph", None),
    )
    graphs, dps = mesh.shape["graph"], mesh.shape["dp"]
    aligned = (128 // (graphs * 2)) % STEP == 0 and graphs >= 4 and mesh.shape["sub"] == 2
    return jax.shard_map(
        fused_body(graphs, dps, mesh.shape["parts"]) if aligned else body,
        mesh=mesh,
        in_specs=placed,
        out_specs=(
            P(("parts", "dp"), "graph", None),
            P(("parts", "dp"), ("graph", "sub"), None),
            P(("parts", "graph", "sub"), None),
            P("parts", ("graph", "sub"), None),
            P("parts", ("graph", "sub"), None),
            P(("parts", "graph", "sub"), None),
            P(("parts", "graph", "sub"), None),
        ),
        check_vma=False,
    )
```

profile of v0, /device:TPU:0, one launch (start us, length us, event | category | flops | bytes accessed | tf_op | source)
XLA Modules:
  0.0 59.7 jit_solution(17502667854191648536)
XLA Ops:
  0.6 0.0 copy-start.7
  0.6 0.7 %copy-done.7 = bf16[128,8]{0,1:T(8,128)(2,1)S(1)} copy-done((bf16[128,8]{0,1:T(8,128)(2,1)S(1)}, bf16[128,8]{0,1:T(8,128)(2,1)}, u32[]{:S(2)}) %copy-start.7) | copy-done | bytes 2072
  1.3 0.0 copy-start.6
  1.3 0.7 %copy.19.refs_8_ = bf16[128,8]{1,0:T(8,128)(2,1)} copy(bf16[128,8]{0,1:T(8,128)(2,1)S(1)} %copy-done.7) | data formatting | bytes 4096 | tf_op args[8]
  2.0 0.0 copy-done.6
  2.0 0.7 %copy.18 = f32[1,160,8]{2,1,0:T(8,128)} copy(f32[1,160,8]{1,2,0:T(8,128)S(1)} %copy-done.6) | data formatting | bytes 10240 | tf_op args[4]
  2.8 50.3 %shard_map.162 = (bf16[16,3200]{1,0:T(8,128)(2,1)}, f32[8,3200]{1,0:T(8,128)}, f32[80,640]{1,0:T(8,128)}, f32[2,64,512]{2,1,0:T(8,128)}, f32[2,48,384]{2,1,0:T(8...) custom-call(bf16[16,3200]{1,0:T(8,128)(2,1)} %bitcast.9, bf16[160,165]{1,0:T(8,128)(2,1)} %bitcast.11, s32[1,160]{1,0:T(1,128)} %refs_2_.1, ...), custom_call_target="tpu_custom_call" | custom-call | tf_op jit(solution)/shard_map/pallas_call | solution.py:917
  53.1 0.0 copy-start.4
  53.1 0.7 %copy-done.4 = f32[16,8]{1,0:T(8,128)S(1)} copy-done((f32[16,8]{1,0:T(8,128)S(1)}, f32[16,8]{1,0:T(8,128)}, u32[]{:S(2)}) %copy-start.4) | copy-done | bytes 536
  53.8 0.0 copy-start.3
  53.8 0.7 %copy.20 = f32[16,8]{0,1:T(8,128)} copy(f32[16,8]{1,0:T(8,128)S(1)} %copy-done.4) | data formatting | bytes 1024
  54.5 0.0 copy-start.1
  54.5 1.6 %copy.27 = bf16[1,16,3200]{2,1,0:T(8,128)(2,1)} copy(bf16[1,16,3200]{2,1,0:T(8,128)(2,1)} %bitcast.8) | data formatting | bytes 204800
  56.0 0.0 copy-done.3
  56.0 0.0 copy-start
  56.0 0.6 %copy.28 = f32[1,8,3200]{2,1,0:T(8,128)} copy(f32[1,8,3200]{2,1,0:T(8,128)S(1)} %bitcast.7) | data formatting | bytes 204800
  56.7 0.0 copy-done.1
  56.7 0.7 %copy.29 = f32[80,640]{1,0:T(8,128)} copy(f32[80,640]{1,0:T(8,128)S(1)} %copy-done.1) | data formatting | bytes 409600
  57.4 0.0 copy-done
  57.4 0.0 copy-start.2
  57.4 0.7 %copy.30 = f32[2,64,512]{2,1,0:T(8,128)} copy(f32[2,64,512]{2,1,0:T(8,128)S(1)} %copy-done) | data formatting | bytes 524288
  58.1 0.3 copy-done.2
  58.4 0.0 copy-start.5
  58.4 0.7 %copy.31 = f32[2,48,384]{2,1,0:T(8,128)} copy(f32[2,48,384]{2,1,0:T(8,128)S(1)} %copy-done.2) | data formatting | bytes 294912
  59.0 0.0 copy-done.5
  59.1 0.6 %copy.32 = f32[16,128]{1,0:T(8,128)} copy(f32[16,128]{1,0:T(8,128)S(1)} %copy-done.5) | data formatting | bytes 16384
Async XLA Ops:
  0.6 0.7 %copy-start.7 = (bf16[128,8]{0,1:T(8,128)(2,1)S(1)}, bf16[128,8]{0,1:T(8,128)(2,1)}, u32[]{:S(2)}) copy-start(bf16[128,8]{0,1:T(8,128)(2,1)} %param.19) | copy-start | bytes 6148
  1.3 0.7 %copy-start.6 = (f32[1,160,8]{1,2,0:T(8,128)S(1)}, f32[1,160,8]{1,2,0:T(8,128)}, u32[]{:S(2)}) copy-start(f32[1,160,8]{1,2,0:T(8,128)} %param.15) | copy-start | bytes 15364
  53.1 0.7 %copy-start.4 = (f32[16,8]{1,0:T(8,128)S(1)}, f32[16,8]{1,0:T(8,128)}, u32[]{:S(2)}) copy-start(f32[16,8]{1,0:T(8,128)} %get-tuple-element.26) | copy-start | bytes 1540
  53.8 2.2 %copy-start.3 = (f32[8,3200]{1,0:T(8,128)S(1)}, f32[8,3200]{1,0:T(8,128)}, u32[]{:S(2)}) copy-start(f32[8,3200]{1,0:T(8,128)} %get-tuple-element.15) | copy-start | bytes 307204
  54.5 2.2 %copy-start.1 = (f32[80,640]{1,0:T(8,128)S(1)}, f32[80,640]{1,0:T(8,128)}, u32[]{:S(2)}) copy-start(f32[80,640]{1,0:T(8,128)} %get-tuple-element.37) | copy-start | bytes 614404
  56.0 1.3 %copy-start = (f32[2,64,512]{2,1,0:T(8,128)S(1)}, f32[2,64,512]{2,1,0:T(8,128)}, u32[]{:S(2)}) copy-start(f32[2,64,512]{2,1,0:T(8,128)} %get-tuple-element.38) | copy-start | bytes 786436
  57.4 1.0 %copy-start.2 = (f32[2,48,384]{2,1,0:T(8,128)S(1)}, f32[2,48,384]{2,1,0:T(8,128)}, u32[]{:S(2)}) copy-start(f32[2,48,384]{2,1,0:T(8,128)} %get-tuple-element.39) | copy-start | bytes 442372
  58.4 0.7 %copy-start.5 = (f32[16,128]{1,0:T(8,128)S(1)}, f32[16,128]{1,0:T(8,128)}, u32[]{:S(2)}) copy-start(f32[16,128]{1,0:T(8,128)} %get-tuple-element.41) | copy-start | bytes 24580
where the time goes:
time: 60 us; the launch traced here: 59.7 us
  Pallas kernels  50.3 us (84%)
  local copies, waits for them, and re-layouts  8.71 us (15%)
  between operations  0.67 us (1%)
    pallas_call x1, Pallas kernels, run(): pl.pallas_call(entry, out_shape=(jax.ShapeDtypeStruct((rows_dev, wide), B...  50.3 us
    unnamed x25, local copies, waits for them, and re-layouts  8.71 us

commit v1 on v0

--- a/solution.py
+++ b/solution.py
@@ -397,16 +397,17 @@
 
 def fused(
     graphs, dps, parts,
-    nf, fr, src, dst, bias, w0, w1, w2, aw, op, go,
-    upd, gn, o0, o1, o2, oa, oproj,
+    nf, fr, src, dst, bias, w0_in, w1_in, w2_in, aw, op, go,
+    upd, gn, tiles_out,
+    w0, w1, w2,
     halo, small, small_in, acc_out, acc_in, fb, gp, sr, mg, zz, vv, weight, bk, gg, ig, rg, ng, ng_in,
     wg, r1, hh, r2, kk, r3, fin,
-    halo_send, halo_recv, small_send, small_recv, acc_send, acc_recv, ng_send, ng_recv,
+    load_sem, halo_send, halo_recv, small_send, small_recv, acc_send, acc_recv, ng_send, ng_recv,
     s1s, s1r, s2s, s2r, s3s, s3r, s4s, s4r,
 ):
     edges = fr.shape[0]
     rows_dev = nf.shape[0]
-    heads = aw.shape[1]
+    heads = aw.shape[0]
     g = lax.axis_index("graph")
     s = lax.axis_index("sub")
     d = lax.axis_index("dp")
@@ -423,6 +424,13 @@
             src_ref=source, dst_ref=target, send_sem=send, recv_sem=recv,
             device_id=device, device_id_type=pl.DeviceIdType.MESH,
         )
+
+    loads = [
+        pltpu.make_async_copy(source, target, load_sem.at[i])
+        for i, (source, target) in enumerate(((w0_in, w0), (w1_in, w1), (w2_in, w2)))
+    ]
+    for load in loads:
+        load.start()
 
     barrier = pltpu.get_barrier_semaphore()
     peers = [{"sub": other}]
@@ -485,7 +493,7 @@
         == jnp.bitwise_and(lax.broadcasted_iota(jnp.int32, (heads, LANES), 1), 7),
         F32,
     )
-    alpha_t = fast(aw[...], tile_heads.astype(BF16)).astype(BF16)
+    alpha_t = inner(aw[...], tile_heads.astype(BF16)).astype(BF16)
     proj = op[...]
 
     for k in range(25):
@@ -535,6 +543,8 @@
 
     lax.fori_loop(0, edges // STEP, rotate_step, 0)
 
+    for load in loads:
+        load.wait()
     z0 = zz[:, lanes(0, 5)]
     zp1, zm1 = zz[:, lanes(5, 4)], zz[:, lanes(9, 4)]
     zp2, zm2 = zz[:, lanes(13, 3)], zz[:, lanes(16, 3)]
@@ -545,9 +555,13 @@
     vv[:, lanes(9, 4)] = (fast(zp1, w1[1]) + fast(zm1, w1[0])).astype(BF16)
     vv[:, lanes(13, 3)] = (fast(zp2, w2[0]) - fast(zm2, w2[1])).astype(BF16)
     vv[:, lanes(16, 3)] = (fast(zp2, w2[1]) + fast(zm2, w2[0])).astype(BF16)
+    bias_lanes = lax.dot_general(
+        bias[...], tile_heads, (((0,), (0,)), ((), ())),
+        preferred_element_type=F32, precision=lax.Precision.HIGHEST,
+    )
     sigmoid = lax.logistic(scalar)
     gate = (scalar * sigmoid).astype(BF16)
-    logits = fast(gate, alpha_t) + exact(bias[...], tile_heads)
+    logits = fast(gate, alpha_t) + bias_lanes
     logits = jnp.where(mine, logits, -1e30)
     product = None
     for k in range(19):
@@ -673,37 +687,65 @@
 
     gp1, gm1 = gg[:, lanes(5, 4)], gg[:, lanes(9, 4)]
     rows1 = 512 // groups
+    one = [None] * 4
+    tiles1 = (rows1 // STEP) * 4
     for b in range(4):
-        zp, zm = zz[:, lanes(5 + b)], zz[:, lanes(9 + b)]
-        base = (rows1 // STEP) * 4
-        put(0, 0, rows1, b * LANES, inner(zp, gp1) + inner(zm, gm1))
-        put(0, base, rows1, b * LANES, inner(zp, gm1) - inner(zm, gp1))
-    zero_tail(0, 2 * (rows1 // STEP) * 4)
-    one = [None] * 3
+        put(0, 0, rows1, b * LANES, inner(zz[:, lanes(5 + b)], gp1) + inner(zz[:, lanes(9 + b)], gm1))
+    zero_tail(0, tiles1)
     one[0] = stage_one(0)
     one[0].start()
+    for b in range(4):
+        put(1, 0, rows1, b * LANES, inner(zz[:, lanes(5 + b)], gm1) - inner(zz[:, lanes(9 + b)], gp1))
+    zero_tail(1, tiles1)
+    one[1] = stage_one(1)
+    one[1].start()
 
     g0 = gg[:, lanes(0, 5)]
     rows0 = 640 // groups
     for b in range(5):
-        put(1, 0, rows0, b * LANES, inner(zz[:, lanes(b)], g0))
+        put(2, 0, rows0, b * LANES, inner(zz[:, lanes(b)], g0))
     alpha_rows = LANES // groups
     tiles0 = (rows0 // STEP) * 5
     logit_small = fast(logit_grad, compact).astype(BF16)
-    put(1, tiles0, alpha_rows, 0, inner(gate, logit_small))
-    zero_tail(1, tiles0 + alpha_rows // STEP)
-    one[1] = stage_one(1)
-    one[1].start()
+    put(2, tiles0, alpha_rows, 0, inner(gate, logit_small))
+    zero_tail(2, tiles0 + alpha_rows // STEP)
+    one[2] = stage_one(2)
+    one[2].start()
+
+    def add_one(piece):
+        one[piece].wait()
+        for p in range(dps):
+            hh[piece][p] = wg[piece][s, p] + r1[piece][p]
+        return start(stage_two(piece))
+
+    def add_two(piece):
+        wait(two[piece])
+        if dps == 2:
+            kk[piece][...] = hh[piece][d] + r2[piece][0]
+        else:
+            value = hh[piece][d].astype(F32)
+            for k in range(1, dps):
+                value = value + r2[piece][k - 1].astype(F32)
+            kk[piece][...] = value.astype(BF16)
+        return start(stage_three(piece))
+
+    def add_three(piece):
+        wait(three[piece])
+        value = kk[piece][g].astype(F32)
+        for k in range(1, graphs):
+            value = value + r3[piece][k - 1].astype(F32)
+        fin[piece][0] = value.astype(BF16)
+        return start(stage_four(piece))
+
+    two = [None] * 4
+    three = [None] * 4
+    four = [None] * 4
+    two[0] = add_one(0)
 
     acc_copy.wait()
     summed = jnp.concatenate(
         [(acc_out[:, lanes(k)] + acc_in[:, lanes(k)]).astype(BF16) for k in range(25)], axis=0
     )
-    projected = fast(summed, proj)
-    for k in range(25):
-        upd[:, lanes(k)] = (
-            nf[:, lanes(k)].astype(F32) + projected[k * rows_dev : (k + 1) * rows_dev]
-        ).astype(BF16)
     cotangent = jnp.concatenate([go[:, lanes(k)] for k in range(25)], axis=0)
     half = rows_dev // 2
     in_half = lax.broadcasted_iota(jnp.int32, summed.shape, 0)
@@ -714,47 +756,21 @@
     tiles2 = (rows2 // STEP) * 3
     for b in range(3):
         zp, zm = zz[:, lanes(13 + b)], zz[:, lanes(16 + b)]
-        put(2, 0, rows2, b * LANES, inner(zp, gp2) + inner(zm, gm2))
-        put(2, tiles2, rows2, b * LANES, inner(zp, gm2) - inner(zm, gp2))
-    put(2, 2 * tiles2, alpha_rows, 0, inner(share, cotangent))
-    zero_tail(2, 2 * tiles2 + alpha_rows // STEP)
-    one[2] = stage_one(2)
-    one[2].start()
-
-    def add_one(piece):
-        one[piece].wait()
-        for p in range(dps):
-            hh[piece][p] = (wg[piece][s, p].astype(F32) + r1[piece][p].astype(F32)).astype(BF16)
-        return start(stage_two(piece))
-
-    def add_two(piece):
-        wait(two[piece])
-        value = hh[piece][d].astype(F32)
-        for k in range(1, dps):
-            value = value + r2[piece][k - 1].astype(F32)
-        kk[piece][...] = value.astype(BF16)
-        return start(stage_three(piece))
-
-    def add_three(piece):
-        wait(three[piece])
-        value = kk[piece][g].astype(F32)
-        for k in range(1, graphs):
-            value = value + r3[piece][k - 1].astype(F32)
-        fin[piece][0] = value.astype(BF16)
-        return start(stage_four(piece))
-
-    two = [None] * 3
-    three = [None] * 3
-    four = [None] * 3
-    two[0] = add_one(0)
+        put(3, 0, rows2, b * LANES, inner(zp, gp2) + inner(zm, gm2))
+        put(3, tiles2, rows2, b * LANES, inner(zp, gm2) - inner(zm, gp2))
+    put(3, 2 * tiles2, alpha_rows, 0, inner(share, cotangent))
+    zero_tail(3, 2 * tiles2 + alpha_rows // STEP)
+    one[3] = stage_one(3)
+    one[3].start()
     two[1] = add_one(1)
 
     ig[:, lanes(0, 5)] = across(g0, w0[...]).astype(BF16)
     ig[:, lanes(5, 4)] = (across(gp1, w1[0]) + across(gm1, w1[1])).astype(BF16)
+    two[2] = add_one(2)
     ig[:, lanes(9, 4)] = (across(gm1, w1[0]) - across(gp1, w1[1])).astype(BF16)
-    two[2] = add_one(2)
     ig[:, lanes(13, 3)] = (across(gp2, w2[0]) + across(gm2, w2[1])).astype(BF16)
     ig[:, lanes(16, 3)] = (across(gm2, w2[0]) - across(gp2, w2[1])).astype(BF16)
+    two[3] = add_one(3)
 
     def row_step(c, _):
         at = pl.ds(pl.multiple_of(c * STEP, STEP), STEP)
@@ -795,6 +811,12 @@
 
     three[0] = add_two(0)
     three[1] = add_two(1)
+
+    projected = fast(summed, proj)
+    for k in range(25):
+        upd[:, lanes(k)] = (
+            nf[:, lanes(k)].astype(F32) + projected[k * rows_dev : (k + 1) * rows_dev]
+        ).astype(BF16)
     three[2] = add_two(2)
 
     wait(node_copies)
@@ -811,33 +833,58 @@
                 base = jnp.where(s == 0, base[:half], base[half:])
                 gn[:, lanes(coef)] = value[part * half : (part + 1) * half] + base
 
-    def take(piece, tile):
+    three[3] = add_two(3)
+    for piece in range(4):
+        four[piece] = add_three(piece)
+    base = 0
+    for piece, count in enumerate(
+        (tiles1, tiles1, tiles0 + alpha_rows // STEP, 2 * tiles2 + alpha_rows // STEP)
+    ):
+        wait(four[piece])
         part = fin[piece].shape[1]
-        slot = lax.rem(d - tile // part + dps, dps)
-        return fin[piece][slot, tile % part].astype(F32)
-
-    four[0] = add_three(0)
-    four[1] = add_three(1)
-    wait(four[0])
+        for p in range(dps):
+            size = min(part, count - p * part)
+            if size > 0:
+                at = base + p * part
+                tiles_out[at : at + size] = fin[piece][lax.rem(d - p + dps, dps), :size]
+        base += count
+
+
+def unpack(upd, gn, tiles, upd_out, gn_out, o0, o1, o2, oa, oproj):
+    upd_out[...] = upd[...]
+    gn_out[...] = gn[...]
+    base = 0
+
+    def matrix(write, rows, wide):
+        nonlocal base
+        for i in range(rows // STEP):
+            for j in range(wide):
+                write(slice(i * STEP, (i + 1) * STEP), lanes(j), tiles[base].astype(F32))
+                base += 1
+
+    def into(ref, lead=None):
+        def write(rows, columns, value):
+            if lead is None:
+                ref[rows, columns] = value
+            else:
+                ref[lead, rows, columns] = value
+
+        return write
+
     for q in range(2):
-        for i in range(rows1 // STEP):
-            for j in range(4):
-                tile = q * (rows1 // STEP) * 4 + i * 4 + j
-                o1[q, i * STEP : (i + 1) * STEP, lanes(j)] = take(0, tile)
-    wait(four[1])
-    for i in range(rows0 // STEP):
-        for j in range(5):
-            o0[i * STEP : (i + 1) * STEP, lanes(j)] = take(1, i * 5 + j)
-    for i in range(alpha_rows // STEP):
-        oa[i * STEP : (i + 1) * STEP, :] = take(1, tiles0 + i)[:, :heads]
-    four[2] = add_three(2)
-    wait(four[2])
+        matrix(into(o1, q), o1.shape[1], 4)
+    matrix(into(o0), o0.shape[0], 5)
+    for i in range(oa.shape[1] // STEP):
+        pick = lax.broadcasted_iota(jnp.int32, (oa.shape[0], LANES), 0) == lax.broadcasted_iota(
+            jnp.int32, (oa.shape[0], LANES), 1
+        )
+        oa[:, i * STEP : (i + 1) * STEP] = across(
+            jnp.where(pick, 1.0, 0.0).astype(BF16), tiles[base]
+        )
+        base += 1
     for q in range(2):
-        for i in range(rows2 // STEP):
-            for j in range(3):
-                o2[q, i * STEP : (i + 1) * STEP, lanes(j)] = take(2, q * tiles2 + i * 3 + j)
-    for i in range(alpha_rows // STEP):
-        oproj[i * STEP : (i + 1) * STEP, :] = take(2, 2 * tiles2 + i)
+        matrix(into(o2, q), o2.shape[1], 3)
+    matrix(into(oproj), oproj.shape[0], 1)
 
 
 def fused_body(graphs, dps, parts):
@@ -848,7 +895,8 @@
         edges = frame_blocks.shape[1]
         heads = alpha_w.shape[1]
         used = (
-            2 * (512 // groups // STEP) * 4,
+            (512 // groups // STEP) * 4,
+            (512 // groups // STEP) * 4,
             (640 // groups // STEP) * 5 + LANES // groups // STEP,
             2 * (384 // groups // STEP) * 3 + LANES // groups // STEP,
         )
@@ -861,6 +909,9 @@
             return [pltpu.VMEM((*lead(p), STEP, LANES), BF16) for p in part]
 
         scratch = [
+            pltpu.VMEM(w_zero.shape, BF16),
+            pltpu.VMEM(w_one.shape, BF16),
+            pltpu.VMEM(w_two.shape, BF16),
             pltpu.VMEM((2, rows_dev, wide), BF16),
             pltpu.VMEM((8, LANES), F32),
             pltpu.VMEM((8, LANES), F32),
@@ -886,11 +937,11 @@
             per_piece(lambda p: (graphs, p)),
             per_piece(lambda p: (graphs - 1, p)),
             per_piece(lambda p: (dps, p)),
-            dma((2,)), dma((2,)), dma, dma, dma, dma, dma((3, 2)), dma((3, 2)),
-            dma((3,)), dma((3,)),
-            dma((3, max(dps - 1, 1))), dma((3, max(dps - 1, 1))),
-            dma((3, graphs - 1)), dma((3, graphs - 1)),
-            dma((3, max(dps - 1, 1))), dma((3, max(dps - 1, 1))),
+            dma((3,)), dma((2,)), dma((2,)), dma, dma, dma, dma, dma((3, 2)), dma((3, 2)),
+            dma((4,)), dma((4,)),
+            dma((4, max(dps - 1, 1))), dma((4, max(dps - 1, 1))),
+            dma((4, graphs - 1)), dma((4, graphs - 1)),
+            dma((4, max(dps - 1, 1))), dma((4, max(dps - 1, 1))),
         ]
         flat = []
         counts = []
@@ -903,7 +954,7 @@
                 flat.append(item)
 
         def entry(*refs):
-            lead, rest = refs[:18], list(refs[18:])
+            lead, rest = refs[:14], list(refs[14:])
             grouped = []
             for count in counts:
                 if count:
@@ -914,28 +965,40 @@
             fused(graphs, dps, parts, *lead, *grouped)
 
         vmem = pl.BlockSpec(memory_space=pltpu.VMEM)
+        anywhere = pl.BlockSpec(memory_space=pl.ANY)
+        count = sum(used)
+        packed = pl.pallas_call(
+            entry,
+            out_shape=(
+                jax.ShapeDtypeStruct((rows_dev, wide), BF16),
+                jax.ShapeDtypeStruct((rows_dev // 2, wide), F32),
+                jax.ShapeDtypeStruct((count, STEP, LANES), BF16),
+            ),
+            in_specs=[vmem] * 5 + [anywhere] * 3 + [vmem] * 3,
+            out_specs=[vmem] * 3,
+            scratch_shapes=flat,
+            compiler_params=pltpu.CompilerParams(
+                collective_id=0, has_side_effects=True, vmem_limit_bytes=56 * 1024 * 1024
+            ),
+        )(
+            node_feats[0], frame_blocks[0], src_ids, dst_ids, edge_bias[0].T,
+            w_zero, w_one, w_two, alpha_w.T, out_proj, grad_out[0],
+        )
         out = pl.pallas_call(
-            entry,
+            unpack,
             out_shape=(
                 jax.ShapeDtypeStruct((rows_dev, wide), BF16),
                 jax.ShapeDtypeStruct((rows_dev // 2, wide), F32),
                 jax.ShapeDtypeStruct((640 // groups, 640), F32),
                 jax.ShapeDtypeStruct((2, 512 // groups, 512), F32),
                 jax.ShapeDtypeStruct((2, 384 // groups, 384), F32),
-                jax.ShapeDtypeStruct((LANES // groups, heads), F32),
+                jax.ShapeDtypeStruct((heads, LANES // groups), F32),
                 jax.ShapeDtypeStruct((LANES // groups, LANES), F32),
             ),
-            in_specs=[vmem] * 11,
+            in_specs=[vmem] * 3,
             out_specs=[vmem] * 7,
-            scratch_shapes=flat,
-            compiler_params=pltpu.CompilerParams(
-                collective_id=0, has_side_effects=True, vmem_limit_bytes=56 * 1024 * 1024
-            ),
-        )(
-            node_feats[0], frame_blocks[0], src_ids, dst_ids, edge_bias[0],
-            w_zero, w_one, w_two, alpha_w, out_proj, grad_out[0],
-        )
-        return (out[0][None], out[1][None], *out[2:])
+        )(*packed)
+        return (out[0][None], out[1][None], out[2], out[3], out[4], out[5].T, out[6])
 
     return run
 

time: 60 us -> 48.9 us (0.81)
  local copies, waits for them, and re-layouts: 8.71 us -> 0 us
  Pallas kernels: 50.3 us -> 48.1 us
    unnamed x25 -> x0, local copies, waits for them, and re-layouts: 8.71 us -> none
    pallas_call x1, Pallas kernels: 50.3 us -> 46.1 us  [run(): pl.pallas_call(entry, out_shape=(jax.ShapeDtypeStruct((rows_dev, wide), B...]
    pallas_call x0 -> x1, Pallas kernels: none -> 1.97 us  [run(): pl.pallas_call(unpack, out_shape=(jax.ShapeDtypeStruct((rows_dev, wide),...]
where the time goes in v1:
time: 48.9 us; the launch traced here: 48.7 us
  Pallas kernels  48.1 us (98%)
  between operations  0.64 us (1%)
    pallas_call x1, Pallas kernels, run(): pl.pallas_call(entry, out_shape=(jax.ShapeDtypeStruct((rows_dev, wide), B...  46.1 us
    pallas_call x1, Pallas kernels, run(): pl.pallas_call(unpack, out_shape=(jax.ShapeDtypeStruct((rows_dev, wide),...  1.97 us

profile of v1, /device:TPU:0, one launch (start us, length us, event | category | flops | bytes accessed | tf_op | source)
XLA Modules:
  0.0 48.7 jit_solution(1851707216617061622)
XLA Ops:
  0.6 46.1 %shard_map.162 = (bf16[16,3200]{1,0:T(8,128)(2,1)}, f32[8,3200]{1,0:T(8,128)}, bf16[77,16,128]{2,1,0:T(8,128)(2,1)}) custom-call(bf16[16,3200]{1,0:T(8,128)(2,1)} %bitcast.10, bf16[160,165]{1,0:T(8,128)(2,1)} %bitcast.12, s32[1,160]{1,0:T(1,128)} %refs_2_.1, s32[1,160]{1,0:T(1,128)} %refs_3_.1, f32[8,160]{1,0:T(8,128)} %bitcast.13, ...), custom_call_target="tpu_custom_call" | custom-call | tf_op jit(solution)/shard_map/pallas_call | solution.py:970
  46.8 2.0 %shard_map.163 = (bf16[16,3200]{1,0:T(8,128)(2,1)}, f32[8,3200]{1,0:T(8,128)}, f32[80,640]{1,0:T(8,128)}, f32[2,64,512]{2,1,0:T(8,128)}, f32[2,48,384]{2,1,0:T(8...) custom-call(bf16[16,3200]{1,0:T(8,128)(2,1)} %get-tuple-element.17.upd, f32[8,3200]{1,0:T(8,128)} %get-tuple-element.18.gn, ...), custom_call_target="tpu_custom_call" | custom-call | tf_op jit(solution)/shard_map/pallas_call | solution.py:987

commit v2 on v1

--- a/solution.py
+++ b/solution.py
@@ -400,7 +400,7 @@
     nf, fr, src, dst, bias, w0_in, w1_in, w2_in, aw, op, go,
     upd, gn, tiles_out,
     w0, w1, w2,
-    halo, small, small_in, acc_out, acc_in, fb, gp, sr, mg, zz, vv, weight, bk, gg, ig, rg, ng, ng_in,
+    halo, small, small_in, acc_out, acc_in, fb, gp, sr, mg, zz, vv, weight, bk, gg, ig, rg, ng, ng_core, ng_sum, ng_in,
     wg, r1, hh, r2, kk, r3, fin,
     load_sem, halo_send, halo_recv, small_send, small_recv, acc_send, acc_recv, ng_send, ng_recv,
     s1s, s1r, s2s, s2r, s3s, s3r, s4s, s4r,
@@ -436,18 +436,19 @@
     peers = [{"sub": other}]
     for k in range(1, graphs):
         peers.append({"graph": along(k)})
-    peers.append({"graph": along(1), "sub": other})
-    peers.append({"graph": along(-1), "sub": other})
     for k in range(1, dps):
         peers.append({"dp": dp_along(k)})
     for peer in peers:
         pl.semaphore_signal(barrier, inc=1, device_id=peer, device_id_type=pl.DeviceIdType.MESH)
     pl.semaphore_wait(barrier, len(peers))
 
-    halo_up = remote(nf, halo.at[0], halo_send.at[0], halo_recv.at[0], {"graph": along(1)})
-    halo_down = remote(nf, halo.at[1], halo_send.at[1], halo_recv.at[1], {"graph": along(-1)})
-    halo_up.start()
-    halo_down.start()
+    section = nf.at[:, pl.ds(pl.multiple_of(s * 12 * LANES, LANES), 13 * LANES)]
+    halos = [
+        remote(section, halo.at[s, i], halo_send.at[i], halo_recv.at[i], {"graph": along(step)})
+        for i, step in enumerate((1, -1))
+    ]
+    for copy in halos:
+        copy.start()
 
     src_row = src[...]
     dst_row = dst[...]
@@ -521,10 +522,19 @@
 
     lax.fori_loop(0, edges // STEP, message_step, 0)
 
-    halo_up.wait()
-    halo_down.wait()
+    shared = [
+        remote(halo.at[s, i], halo.at[s, i], halo_send.at[2 + i], halo_recv.at[2 + i], {"sub": other})
+        for i in range(2)
+    ]
+    for i in range(2):
+        halos[i].wait()
+        shared[i].start()
+    for copy in shared:
+        copy.wait()
     for k in range(25):
-        block = jnp.concatenate([halo[0, :, lanes(k)], nf[:, lanes(k)], halo[1, :, lanes(k)]], axis=0)
+        h = 0 if k < 13 else 1
+        at = lanes(k - 12 * h)
+        block = jnp.concatenate([halo[h, 0, :, at], nf[:, lanes(k)], halo[h, 1, :, at]], axis=0)
         sr[:, lanes(k)] = fast(pick_src, block)
 
     def rotate_step(c, _):
@@ -788,29 +798,24 @@
 
     lax.fori_loop(0, edges // STEP, row_step, 0)
 
+    three[0] = add_two(0)
     for k in range(13):
         low = fast(put_src, rg[:, lanes(k)])
         high = fast(put_src, rg[:, lanes(13 + k)]) if k < 12 else jnp.zeros_like(low)
         for b in range(3):
             for h in range(2):
                 at = slice(b * rows_dev + h * half, b * rows_dev + (h + 1) * half)
-                ng[b, h, :, lanes(k)] = jnp.concatenate([low[at], high[at]], axis=0).astype(BF16)
-    node_copies = []
-    for b in range(3):
-        for r in range(2):
-            if b == 1 and r == 0:
-                continue
-            to = lax.rem(s + r, 2)
-            node_copies.append(
-                remote(
-                    ng.at[b, to], ng_in.at[b, r], ng_send.at[b, r], ng_recv.at[b, r],
-                    {"graph": along(b - 1), "sub": to},
-                )
-            )
+                ng[h, b, :, lanes(k)] = jnp.concatenate([low[at], high[at]], axis=0).astype(BF16)
+    node_core = remote(ng.at[other], ng_core, ng_send.at[0], ng_recv.at[0], {"sub": other})
+    node_core.start()
+    three[1] = add_two(1)
+    node_core.wait()
+    ng_sum[...] = ng[s] + ng_core[...]
+    node_copies = [
+        remote(ng_sum.at[2 * i], ng_in.at[i], ng_send.at[1 + i], ng_recv.at[1 + i], {"graph": along(step)})
+        for i, step in enumerate((-1, 1))
+    ]
     start(node_copies)
-
-    three[0] = add_two(0)
-    three[1] = add_two(1)
 
     projected = fast(summed, proj)
     for k in range(25):
@@ -819,21 +824,17 @@
         ).astype(BF16)
     three[2] = add_two(2)
 
+    three[3] = add_two(3)
     wait(node_copies)
     for k in range(13):
-        value = ng[1, s, :, lanes(k)].astype(F32)
-        for b in range(3):
-            for r in range(2):
-                if b == 1 and r == 0:
-                    continue
-                value = value + ng_in[b, r, :, lanes(k)].astype(F32)
+        value = ng[s, 1, :, lanes(k)].astype(F32) + ng_core[1, :, lanes(k)].astype(F32)
+        value = value + ng_in[0, :, lanes(k)].astype(F32) + ng_in[1, :, lanes(k)].astype(F32)
         for part, coef in ((0, k), (1, 13 + k)):
             if coef < 25:
                 base = go[:, lanes(coef)].astype(F32)
                 base = jnp.where(s == 0, base[:half], base[half:])
                 gn[:, lanes(coef)] = value[part * half : (part + 1) * half] + base
 
-    three[3] = add_two(3)
     for piece in range(4):
         four[piece] = add_three(piece)
     base = 0
@@ -912,7 +913,7 @@
             pltpu.VMEM(w_zero.shape, BF16),
             pltpu.VMEM(w_one.shape, BF16),
             pltpu.VMEM(w_two.shape, BF16),
-            pltpu.VMEM((2, rows_dev, wide), BF16),
+            pltpu.VMEM((2, 2, rows_dev, 13 * LANES), BF16),
             pltpu.VMEM((8, LANES), F32),
             pltpu.VMEM((8, LANES), F32),
             pltpu.VMEM((rows_dev, wide), F32),
@@ -928,8 +929,10 @@
             pltpu.VMEM((edges, kept), BF16),
             pltpu.VMEM((edges, kept), BF16),
             pltpu.VMEM((edges, wide), BF16),
-            pltpu.VMEM((3, 2, STEP, 13 * LANES), BF16),
-            pltpu.VMEM((3, 2, STEP, 13 * LANES), BF16),
+            pltpu.VMEM((2, 3, STEP, 13 * LANES), BF16),
+            pltpu.VMEM((3, STEP, 13 * LANES), BF16),
+            pltpu.VMEM((3, STEP, 13 * LANES), BF16),
+            pltpu.VMEM((2, STEP, 13 * LANES), BF16),
             per_piece(lambda p: (2, dps, graphs, p)),
             per_piece(lambda p: (dps, graphs, p)),
             per_piece(lambda p: (dps, graphs, p)),
@@ -937,7 +940,7 @@
             per_piece(lambda p: (graphs, p)),
             per_piece(lambda p: (graphs - 1, p)),
             per_piece(lambda p: (dps, p)),
-            dma((3,)), dma((2,)), dma((2,)), dma, dma, dma, dma, dma((3, 2)), dma((3, 2)),
+            dma((3,)), dma((4,)), dma((4,)), dma, dma, dma, dma, dma((3,)), dma((3,)),
             dma((4,)), dma((4,)),
             dma((4, max(dps - 1, 1))), dma((4, max(dps - 1, 1))),
             dma((4, graphs - 1)), dma((4, graphs - 1)),

time: 48.9 us -> 46.9 us (0.959)
  Pallas kernels: 48.1 us -> 46.1 us
    pallas_call x1, Pallas kernels: 46.1 us -> 44.1 us  [run(): pl.pallas_call(entry, out_shape=(jax.ShapeDtypeStruct((rows_dev, wide), B...]
where the time goes in v2:
time: 46.9 us; the launch traced here: 46.7 us
  Pallas kernels  46.1 us (98%)
  between operations  0.64 us (1%)
    pallas_call x1, Pallas kernels, run(): pl.pallas_call(entry, out_shape=(jax.ShapeDtypeStruct((rows_dev, wide), B...  44.1 us
    pallas_call x1, Pallas kernels, run(): pl.pallas_call(unpack, out_shape=(jax.ShapeDtypeStruct((rows_dev, wide),...  1.97 us

profile of v2, /device:TPU:0, one launch (start us, length us, event | category | flops | bytes accessed | tf_op | source)
XLA Modules:
  0.0 46.7 jit_solution(5550058328227989209)
XLA Ops:
  0.6 44.1 %shard_map.162 = (bf16[16,3200]{1,0:T(8,128)(2,1)}, f32[8,3200]{1,0:T(8,128)}, bf16[77,16,128]{2,1,0:T(8,128)(2,1)}) custom-call(bf16[16,3200]{1,0:T(8,128)(2,1)} %bitcast.10, bf16[160,165]{1,0:T(8,128)(2,1)} %bitcast.12, s32[1,160]{1,0:T(1,128)} %refs_2_.1, s32[1,160]{1,0:T(1,128)} %refs_3_.1, f32[8,160]{1,0:T(8,128)} %bitcast.13, ...), custom_call_target="tpu_custom_call" | custom-call | tf_op jit(solution)/shard_map/pallas_call | solution.py:973
  44.8 2.0 %shard_map.163 = (bf16[16,3200]{1,0:T(8,128)(2,1)}, f32[8,3200]{1,0:T(8,128)}, f32[80,640]{1,0:T(8,128)}, f32[2,64,512]{2,1,0:T(8,128)}, f32[2,48,384]{2,1,0:T(8...) custom-call(bf16[16,3200]{1,0:T(8,128)(2,1)} %get-tuple-element.17.upd, f32[8,3200]{1,0:T(8,128)} %get-tuple-element.18.gn, ...), custom_call_target="tpu_custom_call" | custom-call | tf_op jit(solution)/shard_map/pallas_call | solution.py:990

commit v3 on v2

--- a/solution.py
+++ b/solution.py
@@ -697,7 +697,7 @@
 
     gp1, gm1 = gg[:, lanes(5, 4)], gg[:, lanes(9, 4)]
     rows1 = 512 // groups
-    one = [None] * 4
+    one = [None] * 5
     tiles1 = (rows1 // STEP) * 4
     for b in range(4):
         put(0, 0, rows1, b * LANES, inner(zz[:, lanes(5 + b)], gp1) + inner(zz[:, lanes(9 + b)], gm1))
@@ -747,9 +747,9 @@
         fin[piece][0] = value.astype(BF16)
         return start(stage_four(piece))
 
-    two = [None] * 4
-    three = [None] * 4
-    four = [None] * 4
+    two = [None] * 5
+    three = [None] * 5
+    four = [None] * 5
     two[0] = add_one(0)
 
     acc_copy.wait()
@@ -765,14 +765,17 @@
     rows2 = 384 // groups
     tiles2 = (rows2 // STEP) * 3
     for b in range(3):
-        zp, zm = zz[:, lanes(13 + b)], zz[:, lanes(16 + b)]
-        put(3, 0, rows2, b * LANES, inner(zp, gp2) + inner(zm, gm2))
-        put(3, tiles2, rows2, b * LANES, inner(zp, gm2) - inner(zm, gp2))
-    put(3, 2 * tiles2, alpha_rows, 0, inner(share, cotangent))
-    zero_tail(3, 2 * tiles2 + alpha_rows // STEP)
+        put(3, 0, rows2, b * LANES, inner(zz[:, lanes(13 + b)], gp2) + inner(zz[:, lanes(16 + b)], gm2))
+    zero_tail(3, tiles2)
     one[3] = stage_one(3)
     one[3].start()
     two[1] = add_one(1)
+    for b in range(3):
+        put(4, 0, rows2, b * LANES, inner(zz[:, lanes(13 + b)], gm2) - inner(zz[:, lanes(16 + b)], gp2))
+    put(4, tiles2, alpha_rows, 0, inner(share, cotangent))
+    zero_tail(4, tiles2 + alpha_rows // STEP)
+    one[4] = stage_one(4)
+    one[4].start()
 
     ig[:, lanes(0, 5)] = across(g0, w0[...]).astype(BF16)
     ig[:, lanes(5, 4)] = (across(gp1, w1[0]) + across(gm1, w1[1])).astype(BF16)
@@ -781,6 +784,7 @@
     ig[:, lanes(13, 3)] = (across(gp2, w2[0]) + across(gm2, w2[1])).astype(BF16)
     ig[:, lanes(16, 3)] = (across(gm2, w2[0]) - across(gp2, w2[1])).astype(BF16)
     two[3] = add_one(3)
+    two[4] = add_one(4)
 
     def row_step(c, _):
         at = pl.ds(pl.multiple_of(c * STEP, STEP), STEP)
@@ -825,6 +829,8 @@
     three[2] = add_two(2)
 
     three[3] = add_two(3)
+    four[0] = add_three(0)
+    three[4] = add_two(4)
     wait(node_copies)
     for k in range(13):
         value = ng[s, 1, :, lanes(k)].astype(F32) + ng_core[1, :, lanes(k)].astype(F32)
@@ -835,11 +841,11 @@
                 base = jnp.where(s == 0, base[:half], base[half:])
                 gn[:, lanes(coef)] = value[part * half : (part + 1) * half] + base
 
-    for piece in range(4):
+    for piece in range(1, 5):
         four[piece] = add_three(piece)
     base = 0
     for piece, count in enumerate(
-        (tiles1, tiles1, tiles0 + alpha_rows // STEP, 2 * tiles2 + alpha_rows // STEP)
+        (tiles1, tiles1, tiles0 + alpha_rows // STEP, tiles2, tiles2 + alpha_rows // STEP)
     ):
         wait(four[piece])
         part = fin[piece].shape[1]
@@ -899,7 +905,8 @@
             (512 // groups // STEP) * 4,
             (512 // groups // STEP) * 4,
             (640 // groups // STEP) * 5 + LANES // groups // STEP,
-            2 * (384 // groups // STEP) * 3 + LANES // groups // STEP,
+            (384 // groups // STEP) * 3,
+            (384 // groups // STEP) * 3 + LANES // groups // STEP,
         )
         part = [-(-count // dps) for count in used]
         dma = pltpu.SemaphoreType.DMA
@@ -941,10 +948,10 @@
             per_piece(lambda p: (graphs - 1, p)),
             per_piece(lambda p: (dps, p)),
             dma((3,)), dma((4,)), dma((4,)), dma, dma, dma, dma, dma((3,)), dma((3,)),
-            dma((4,)), dma((4,)),
-            dma((4, max(dps - 1, 1))), dma((4, max(dps - 1, 1))),
-            dma((4, graphs - 1)), dma((4, graphs - 1)),
-            dma((4, max(dps - 1, 1))), dma((4, max(dps - 1, 1))),
+            dma((5,)), dma((5,)),
+            dma((5, max(dps - 1, 1))), dma((5, max(dps - 1, 1))),
+            dma((5, graphs - 1)), dma((5, graphs - 1)),
+            dma((5, max(dps - 1, 1))), dma((5, max(dps - 1, 1))),
         ]
         flat = []
         counts = []

time: 46.9 us -> 47.2 us (level)
  no operation moved by 1% of the time
where the time goes in v3:
time: 47.2 us; the launch traced here: 47 us
  Pallas kernels  46.4 us (98%)
  between operations  0.64 us (1%)
    pallas_call x1, Pallas kernels, run(): pl.pallas_call(entry, out_shape=(jax.ShapeDtypeStruct((rows_dev, wide), B...  44.4 us
    pallas_call x1, Pallas kernels, run(): pl.pallas_call(unpack, out_shape=(jax.ShapeDtypeStruct((rows_dev, wide),...  1.97 us

profile of v3, /device:TPU:0, one launch (start us, length us, event | category | flops | bytes accessed | tf_op | source)
XLA Modules:
  0.0 47.0 jit_solution(17203040948162458964)
XLA Ops:
  0.6 44.4 %shard_map.162 = (bf16[16,3200]{1,0:T(8,128)(2,1)}, f32[8,3200]{1,0:T(8,128)}, bf16[77,16,128]{2,1,0:T(8,128)(2,1)}) custom-call(bf16[16,3200]{1,0:T(8,128)(2,1)} %bitcast.10, bf16[160,165]{1,0:T(8,128)(2,1)} %bitcast.12, s32[1,160]{1,0:T(1,128)} %refs_2_.1, s32[1,160]{1,0:T(1,128)} %refs_3_.1, f32[8,160]{1,0:T(8,128)} %bitcast.13, ...), custom_call_target="tpu_custom_call" | custom-call | tf_op jit(solution)/shard_map/pallas_call | solution.py:980
  45.0 2.0 %shard_map.163 = (bf16[16,3200]{1,0:T(8,128)(2,1)}, f32[8,3200]{1,0:T(8,128)}, f32[80,640]{1,0:T(8,128)}, f32[2,64,512]{2,1,0:T(8,128)}, f32[2,48,384]{2,1,0:T(8...) custom-call(bf16[16,3200]{1,0:T(8,128)(2,1)} %get-tuple-element.17.upd, f32[8,3200]{1,0:T(8,128)} %get-tuple-element.18.gn, ...), custom_call_target="tpu_custom_call" | custom-call | tf_op jit(solution)/shard_map/pallas_call | solution.py:997
